TPU v7x, 32 devices: a whole 2x2x4 slice. The times are simulated.
32 devices in a mesh: copy: 16 (over z, y, core), table: 2 (over x).
Axes of the slice: x: 2, y: 2, z: 4, core: 2. Of those that a mesh axis runs over, the one named last changes fastest.
Arguments:
- pooled: bfloat16 [4096, 28, 128], P('copy', 'table'), may hold values from -6 to 6
- slot_of_table: int32 [26], replicated, may hold values from 0 to 27, as said below
- partner: int32 [16], replicated, may hold values from 0 to 15, as said below
- labels: int32 [4096], P('copy'), may hold values 0 or 1
- w_first: bfloat16 [16, 3328, 4096], P('copy', None, 'table'), may hold values from -0.109375 to 0.109375
- b_first: bfloat16 [16, 4096], P('copy', 'table'), may hold values from -3 to 3
- w_head: bfloat16 [16, 4096], P('copy', 'table'), may hold values from -0.1875 to 0.1875
Outputs:
- pooled_grad: bfloat16 [28, 128, 4096], P('table', None, 'copy')
- grad_first: bfloat16 [16, 3328, 4096], P('copy', None, 'table')
- grad_bias: float32 [16, 4096], P('copy', 'table')
- grad_head: float32 [16, 4096], P('copy', 'table')
- loss_mean: float32 [16], P('copy')
Inputs may be any that keep to these rules, and one draw needn't show every extreme that they name: The slots are distinct; table t lies on the device of index slot_of_table[t] // 14 of the table axis; slots 0 and 27 are always used. A pairing: partner[partner[c]] == c and partner[c] != c.
All inputs are finite; a program needn't handle non-finite values. No bound on the sum of `labels` on one device may be relied on, other than what follows from the above.
Results may differ from a plain program's by a relative error of at most 0.017.
Values may be sent and summed in bfloat16 or wider, within the bound.
No kernel may reach another device: no remote copies, remote signals or barrier semaphores. Data moves between devices by JAX's collectives and lax.ppermute only.
A program may use at most 192 MiB of HBM per device.

v0:
```python
import functools

import jax
import jax.numpy as jnp
from jax import lax
from jax.experimental import pallas as pl
from jax.experimental.pallas import tpu as pltpu
from jax.sharding import PartitionSpec as P

VMEM_LIMIT = 24 * 1024 * 1024
VMEM = pl.BlockSpec(memory_space=pltpu.VMEM)
SMEM = pl.BlockSpec(memory_space=pltpu.SMEM)
HBM = pl.BlockSpec(memory_space=pltpu.HBM)
TILE = 256


def in_hbm(value):
    return pltpu.with_memory_space_constraint(value, pltpu.HBM)


def whole(shape):
    return pl.BlockSpec(shape, lambda *_: (0,) * len(shape))


def tiles(width):
    return TILE if width % TILE == 0 else width


def part_of(i, size):
    return pl.ds(pl.multiple_of(i * size, size), size)


def copy_features(slot_of, blocks, feats):
    me, tables = lax.axis_index("table"), lax.axis_size("table")
    emb = blocks[0][0].shape[2]
    slots = sum(piece.shape[0] for piece in blocks[0])

    @pl.loop(0, feats.shape[1] // emb)
    def _(t):
        slot = slot_of[t]
        place = lax.rem(slot, slots)
        group = lax.rem(me + tables - slot // slots, tables)
        for k, pieces in enumerate(blocks):
            first = 0
            for piece in pieces:
                last = first + piece.shape[0]

                @pl.when((group == k) & (place >= first) & (place < last))
                def _():
                    feats[:, part_of(t, emb)] = piece[place - first]

                first = last


def forward_tiles(feats, w, b, held, finish, arrive=lambda i: None):
    tile = held.shape[1]
    count = w.shape[1] // tile

    def product(i):
        arrive(i)
        cut = part_of(i, tile)
        value = jnp.dot(feats[...], w[:, cut], preferred_element_type=jnp.float32)
        return value + b[:, cut].astype(jnp.float32)

    held[...] = product(0)

    @pl.loop(1, count)
    def _(i):
        before = held[...]
        value = product(i)
        finish(i - 1, before)
        held[...] = value

    finish(count - 1, held[...])


def swish(pre):
    sigmoid = 0.5 * jnp.tanh(0.5 * pre) + 0.5
    return sigmoid, pre * sigmoid


def add_lanes(total, wide):
    for lane in range(0, wide.shape[1], 128):
        total[...] += wide[:, lane : lane + 128]


def student_body(count, slot_of, *refs):
    given, others, refs = refs[:4], refs[4 : 3 + count], refs[3 + count :]
    logit, slope, active, feats, w, *refs = refs
    grads, (held, total, turned, own, b, h, here, arrived) = refs[:count], refs[count:]
    slots, emb, _ = grads[0].shape
    tile = held.shape[1]
    small = [
        pltpu.make_async_copy(source, here_now, here.at[i])
        for i, (source, here_now) in enumerate(zip(given[1:], (own, b, h)))
    ]
    for copy in small:
        copy.start()

    def fetch(i):
        cut = part_of(i, tile)
        return pltpu.make_async_copy(given[0].at[:, cut], w.at[:, cut], arrived.at[i])

    @pl.loop(0, w.shape[1] // tile)
    def _(i):
        fetch(i).start()

    for copy in small:
        copy.wait()
    copy_features(slot_of, [[own]] + [[other] for other in others], feats)
    total[...] = jnp.zeros_like(total)

    def finish(i, pre):
        cut = part_of(i, pre.shape[1])
        head = h[:, cut].astype(jnp.float32)
        sigmoid, act = swish(pre)
        add_lanes(total, act * head)
        low = (head * (sigmoid + act * (1.0 - sigmoid))).astype(jnp.bfloat16)
        slope[:, cut] = low
        turned[cut, :] = low.T
        active[:, cut] = act.astype(jnp.bfloat16)

    forward_tiles(feats, w, b, held, finish, lambda i: fetch(i).wait())
    logit[...] = jnp.sum(total[...].T, axis=0, keepdims=True)

    for grad in grads:
        grad[...] = jnp.zeros_like(grad)

    me, tables = lax.axis_index("table"), lax.axis_size("table")
    used = w.shape[0] // emb
    group = max(n for n in range(1, 14) if used % n == 0)

    @pl.loop(0, used // group)
    def _(i):
        value = jnp.dot(
            w[part_of(i, group * emb), :], turned[...], preferred_element_type=jnp.float32
        ).astype(jnp.bfloat16)
        for j in range(group):
            slot = slot_of[group * i + j]
            owner = lax.rem(slot // slots + tables - me, tables)
            for k, grad in enumerate(grads):

                @pl.when(owner == k)
                def _():
                    grad[lax.rem(slot, slots)] = value[j * emb : (j + 1) * emb, :]


def student(slot_of, blocks, w, b, h):
    slots, rows, emb = blocks[0].shape
    depth, units = w.shape
    count = len(blocks)
    shape = jax.ShapeDtypeStruct
    return pl.pallas_call(
        functools.partial(student_body, count),
        in_specs=[SMEM] + [HBM] * 4 + [VMEM] * (count - 1),
        out_specs=[VMEM] * (5 + count),
        out_shape=[
            shape((1, rows), jnp.float32),
            shape((rows, units), jnp.bfloat16),
            shape((rows, units), jnp.bfloat16),
            shape((rows, depth), jnp.bfloat16),
            shape((depth, units), jnp.bfloat16),
        ]
        + [shape((slots, emb, rows), jnp.bfloat16)] * count,
        scratch_shapes=[
            pltpu.VMEM((rows, tiles(units)), jnp.float32),
            pltpu.VMEM((rows, 128), jnp.float32),
            pltpu.VMEM((units, rows), jnp.bfloat16),
            pltpu.VMEM((slots, rows, emb), jnp.bfloat16),
            pltpu.VMEM((1, units), jnp.bfloat16),
            pltpu.VMEM((1, units), jnp.bfloat16),
            pltpu.SemaphoreType.DMA((3,)),
            pltpu.SemaphoreType.DMA((units // tiles(units),)),
        ],
        compiler_params=pltpu.CompilerParams(vmem_limit_bytes=VMEM_LIMIT),
        cost_estimate=pl.CostEstimate(
            flops=4 * rows * depth * units,
            bytes_accessed=2 * depth * units,
            transcendentals=rows * units,
        ),
    )(slot_of, *(in_hbm(x) for x in (w, blocks[0], b, h)), *blocks[1:])


def teacher_body(pieces, slot_of, *refs):
    count = sum(pieces)
    blocks, (w, b, h, logit, feats, held, total) = list(refs[:count]), refs[count:]
    copy_features(slot_of, [[blocks.pop(0) for _ in range(n)] for n in pieces], feats)
    total[...] = jnp.zeros_like(total)

    def finish(i, pre):
        head = h[:, part_of(i, pre.shape[1])].astype(jnp.float32)
        add_lanes(total, swish(pre)[1] * head)

    forward_tiles(feats, w, b, held, finish)
    logit[...] = jnp.sum(total[...].T, axis=0, keepdims=True)


def teacher(slot_of, blocks, w, b, h):
    rows = blocks[0][0].shape[1]
    depth, units = w.shape
    pieces = [len(block) for block in blocks]
    count = sum(pieces)
    return pl.pallas_call(
        functools.partial(teacher_body, pieces),
        in_specs=[SMEM] + [VMEM] * (count + 3),
        out_specs=VMEM,
        out_shape=jax.ShapeDtypeStruct((1, rows), jnp.float32),
        scratch_shapes=[
            pltpu.VMEM((rows, depth), jnp.bfloat16),
            pltpu.VMEM((rows, tiles(units)), jnp.float32),
            pltpu.VMEM((rows, 128), jnp.float32),
        ],
        compiler_params=pltpu.CompilerParams(vmem_limit_bytes=VMEM_LIMIT),
        cost_estimate=pl.CostEstimate(
            flops=2 * rows * depth * units,
            bytes_accessed=2 * depth * units,
            transcendentals=rows * units,
        ),
    )(slot_of, *(piece for block in blocks for piece in block), w, b, h)


def rows_body(count, y_ref, *refs):
    zs, ts, refs = refs[:count], refs[count : 2 * count], refs[2 * count :]
    slope, active, low, bias, head, loss, scale = refs
    rows = y_ref.shape[1]
    z = sum(ref[...] for ref in zs)
    soft = jax.nn.sigmoid(sum(ref[...] for ref in ts))
    y = y_ref[...].astype(jnp.float32)
    grads = 2.0 * jax.nn.sigmoid(z) - y - soft
    scale[...] = grads
    softplus = jnp.maximum(z, 0.0) + jnp.log1p(jnp.exp(-jnp.abs(z)))
    losses = 2.0 * softplus - y * z - soft * z
    loss[...] = jnp.sum(losses, axis=1, keepdims=True) / rows
    column = jnp.broadcast_to(grads, (128, rows)).T

    @pl.loop(0, slope.shape[1] // 128)
    def _(i):
        cut = part_of(i, 128)
        pre = slope[:, cut].astype(jnp.float32) * column
        low[:, cut] = pre.astype(jnp.bfloat16)
        bias[:, cut] = jnp.sum(pre, axis=0, keepdims=True)
        head[:, cut] = jnp.sum(
            active[:, cut].astype(jnp.float32) * column, axis=0, keepdims=True
        )


def row_grads(z_parts, t_parts, labels, slope, active):
    rows, units = slope.shape
    shape = jax.ShapeDtypeStruct
    row, units_row = whole((1, rows)), whole((1, units))
    return pl.pallas_call(
        functools.partial(rows_body, len(z_parts)),
        grid=(1,),
        in_specs=[row] * (1 + len(z_parts) + len(t_parts)) + [VMEM] * 2,
        out_specs=[VMEM, units_row, units_row, whole((1, 1)), row],
        out_shape=[
            shape((rows, units), jnp.bfloat16),
            shape((1, units), jnp.float32),
            shape((1, units), jnp.float32),
            shape((1, 1), jnp.float32),
            shape((1, rows), jnp.float32),
        ],
        compiler_params=pltpu.CompilerParams(vmem_limit_bytes=VMEM_LIMIT),
    )(labels, *z_parts, *t_parts, slope, active)


def scaled_body(count, scale, *refs):
    total = sum(ref[...].astype(jnp.float32) for ref in refs[:count])
    refs[count][...] = (total * scale[...]).astype(jnp.bfloat16)


def scaled_sum(scale, parts):
    slots, emb, rows = parts[0].shape
    group = 7 if slots % 7 == 0 else slots
    block = pl.BlockSpec((group, emb, rows), lambda i: (i, 0, 0))
    return pl.pallas_call(
        functools.partial(scaled_body, len(parts)),
        grid=(slots // group,),
        in_specs=[whole((1, 1, rows))] + [block] * len(parts),
        out_specs=block,
        out_shape=jax.ShapeDtypeStruct((slots, emb, rows), jnp.bfloat16),
        compiler_params=pltpu.CompilerParams(vmem_limit_bytes=VMEM_LIMIT),
    )(scale.reshape(1, 1, rows), *parts)


def across(value, shift):
    count = lax.axis_size("table")
    return lax.ppermute(value, "table", [(i, (i + shift) % count) for i in range(count)])


def swap(bits, value, shift=0):
    copies, tables = lax.axis_size("copy"), lax.axis_size("table")
    pairs = [
        (c * tables + i, (c ^ bits) * tables + (i + shift) % tables)
        for c in range(copies)
        for i in range(tables)
    ]
    return lax.ppermute(value, ("copy", "table"), pairs)


def after(value, other):
    return lax.optimization_barrier((value, other))[0]


def by_distance(run, distance, *values):
    branches = [functools.partial(run, bits) for bits in range(1, lax.axis_size("copy"))]
    return lax.switch(distance - 1, branches, *values)


def swap_logits(bits, z_own, t_own):
    shifts = range(lax.axis_size("table"))
    t_parts = [swap(bits, t_own, k) for k in shifts]
    return [z_own] + [across(z_own, k) for k in shifts if k], t_parts


def on_device(pooled, slot_of_table, partner, labels, w_first, b_first, w_head):
    tables = lax.axis_size("table")
    rows, slots, emb = pooled.shape
    me_copy = lax.axis_index("copy")
    distance = jnp.bitwise_xor(me_copy, partner[me_copy])

    own = jnp.transpose(pooled, (1, 0, 2))
    blocks = [own] + [across(own, k) for k in range(1, tables)]
    cuts = [0, (5 * slots) // 7, slots] if slots % 7 == 0 else [0, slots]
    theirs = []
    for first, last in zip(cuts, cuts[1:]):
        piece = own[first:last]
        if theirs:
            piece = after(piece, theirs[-1])
        theirs.append(by_distance(swap, distance, piece))
    their_blocks = [theirs] + [[across(piece, k) for piece in theirs] for k in range(1, tables)]

    z_own, slope, active, feats, w, *parts = student(
        slot_of_table, blocks, w_first[0], b_first, w_head
    )
    parts = parts[:1] + [across(part, k) for k, part in enumerate(parts) if k]
    t_own = teacher(slot_of_table, their_blocks, w, b_first, w_head)
    z_parts, t_parts = by_distance(swap_logits, distance, z_own, t_own)

    low, grad_bias, grad_head, loss, scale = row_grads(
        z_parts, t_parts, labels.reshape(1, rows), slope, active
    )
    grad_first = lax.dot_general(
        feats, low, (((0,), (0,)), ((), ())), preferred_element_type=jnp.float32
    ).astype(jnp.bfloat16)
    pooled_grad = scaled_sum(scale, parts)
    return (pooled_grad, grad_first[None], grad_bias, grad_head, loss.reshape(1))


def solution(mesh):
    in_specs = (
        P("copy", "table", None),
        P(),
        P(),
        P("copy"),
        P("copy", None, "table"),
        P("copy", "table"),
        P("copy", "table"),
    )
    out_specs = (
        P("table", None, "copy"),
        P("copy", None, "table"),
        P("copy", "table"),
        P("copy", "table"),
        P("copy"),
    )
    return jax.shard_map(
        on_device, mesh=mesh, in_specs=in_specs, out_specs=out_specs, check_vma=False
    )
```

profile of v0, /device:TPU:16, one launch (start us, length us, event | category | flops | bytes accessed | tf_op | source)
XLA Modules:
  0.0 95.9 jit_solution(6693677384628987724)
XLA Ops:
  0.6 1.6 %collective-permute-start.75 = (bf16[14,256,128]{2,1,0:T(8,128)(2,1)}, bf16[14,256,128]{2,1,0:T(8,128)(2,1)S(1)}, u32[]{:S(2)}, u32[]{:S(2)}) collective-permute-start(bf16[14,256,128]{2,1,0:T(8,128)(2,1)} %bitcast.12), channel_id=1, source_target_pairs={{0,1},{1,0},{2,3},{3,2},{4,5},{5,4},{6,7},{7,6},{8,9},{9,8},{10,11... | collective-permute-start | bytes 2752520 | tf_op jit(solution)/shard_map/ppermute | solution.py:288
  2.2 0.0 copy-start.5
  2.2 1.2 %slice.53 = bf16[10,256,128]{2,1,0:T(8,128)(2,1)S(1)} slice(bf16[14,256,128]{2,1,0:T(8,128)(2,1)} %bitcast.13), slice={[0:10], [0:256], [0:128]} | slice | bytes 1310720 | tf_op jit(solution)/shard_map/slice | solution.py:327
  3.4 1.2 %dynamic_slice.3 = s32[1]{0:T(128)} dynamic-slice(s32[16]{0:T(128)} %param.54, s32[]{:T(128)S(6)} %select_n.3), dynamic_slice_sizes={1} | dynamic-slice | bytes 12 | tf_op jit(solution)/shard_map/dynamic_slice | solution.py:320
  5.3 28.6 %conditional.3 = (bf16[10,256,128]{2,1,0:T(8,128)(2,1)}) conditional(s32[]{:T(128)} %clamp.2, bf16[10,256,128]{2,1,0:T(8,128)(2,1)S(1)} %slice.53, bf16[10,256,128]{2,1,0:T(8,128)(2,1)S(1)} %slice.53, bf16[10,256,128]{2,1,0:T(8,128)(2,1)S(1)} %slice.53, bf16[10,256,128]{2,1,0:T(8,128)(2,1)S(1)} %slice.53, ...), branch_computations={%region_0.0_spmd, %region_1.0_spmd, %region_2.0_spmd, %region_3.0_... | conditional | bytes 2621488 | solution.py:307
  5.3 1.4 %collective-permute-start.9 = (bf16[10,256,128]{2,1,0:T(8,128)(2,1)S(1)}, bf16[10,256,128]{2,1,0:T(8,128)(2,1)}, u32[]{:S(2)}, u32[]{:S(2)}) collective-permute-start(bf16[10,256,128]{2,1,0:T(8,128)(2,1)S(1)} %param.9), channel_id=1, source_target_pairs={{0,20},{1,21},{2,22},{3,23},{4,16},{5,17},{6,18},{7,19},{8,28},{9,... | collective-permute-start | bytes 1966088 | tf_op jit(solution)/shard_map/cond/branch_9_fun/ppermute | solution.py:298
  6.6 27.2 %collective-permute-done.9 = bf16[10,256,128]{2,1,0:T(8,128)(2,1)} collective-permute-done((bf16[10,256,128]{2,1,0:T(8,128)(2,1)S(1)}, bf16[10,256,128]{2,1,0:T(8,128)(2,1)}, u32[]{:S(2)}, u32[]{:S(2)}) %collective-permute-start.9) | collective-permute-done | bytes 655392 | tf_op jit(solution)/shard_map/cond/branch_9_fun/ppermute | solution.py:298
  33.9 0.5 collective-permute-start.76
  34.4 1.0 %slice.54 = bf16[4,256,128]{2,1,0:T(8,128)(2,1)S(1)} slice(bf16[14,256,128]{2,1,0:T(8,128)(2,1)} %bitcast.14), slice={[10:14], [0:256], [0:128]} | slice | bytes 524288 | tf_op jit(solution)/shard_map/slice | solution.py:327
  35.4 8.9 %conditional.4 = (bf16[4,256,128]{2,1,0:T(8,128)(2,1)}) conditional(s32[]{:T(128)} %clamp.2, bf16[4,256,128]{2,1,0:T(8,128)(2,1)S(1)} %slice.54, bf16[4,256,128]{2,1,0:T(8,128)(2,1)S(1)} %slice.54, bf16[4,256,128]{2,1,0:T(8,128)(2,1)S(1)} %slice.54, bf16[4,256,128]{2,1,0:T(8,128)(2,1)S(1)} %slice.54, ...), branch_computations={%region_15.0_spmd, %region_16.0_spmd, %region_17.0_spmd, %region_1... | conditional | bytes 1048624 | solution.py:307
  35.4 4.4 %collective-permute-start.24 = (bf16[4,256,128]{2,1,0:T(8,128)(2,1)S(1)}, bf16[4,256,128]{2,1,0:T(8,128)(2,1)}, u32[]{:S(2)}, u32[]{:S(2)}) collective-permute-start(bf16[4,256,128]{2,1,0:T(8,128)(2,1)S(1)} %param.24), channel_id=1, source_target_pairs={{0,20},{1,21},{2,22},{3,23},{4,16},{5,17},{6,18},{7,19},{8,28},{9,... | collective-permute-start | bytes 786440 | tf_op jit(solution)/shard_map/cond/branch_9_fun/ppermute | solution.py:298
  39.9 4.5 %collective-permute-done.24 = bf16[4,256,128]{2,1,0:T(8,128)(2,1)} collective-permute-done((bf16[4,256,128]{2,1,0:T(8,128)(2,1)S(1)}, bf16[4,256,128]{2,1,0:T(8,128)(2,1)}, u32[]{:S(2)}, u32[]{:S(2)}) %collective-permute-start.24) | collective-permute-done | bytes 262176 | tf_op jit(solution)/shard_map/cond/branch_9_fun/ppermute | solution.py:298
  44.3 1.5 %collective-permute-start.77 = (bf16[4,256,128]{2,1,0:T(8,128)(2,1)}, bf16[4,256,128]{2,1,0:T(8,128)(2,1)S(1)}, u32[]{:S(2)}, u32[]{:S(2)}) collective-permute-start(bf16[4,256,128]{2,1,0:T(8,128)(2,1)} %get-tuple-element.235.refs_1_), channel_id=1, source_target_pairs={{0,1},{1,0},{2,3},{3,2},{4,5},{5,4},{6,7},{7,6},{8,9},{9,8},{10,11... | collective-permute-start | bytes 786440 | tf_op jit(solution)/shard_map/ppermute | solution.py:288
  45.8 0.0 collective-permute-done.75.refs_4_
  45.8 0.0 copy-start.8
  45.8 0.9 copy-done.8
  46.8 0.0 copy-start.7
  46.8 0.7 copy-done.7
  47.4 0.0 copy-start.9
  47.4 1.2 %copy-done.9 = bf16[14,256,128]{2,1,0:T(8,128)(2,1)S(1)} copy-done((bf16[14,256,128]{2,1,0:T(8,128)(2,1)S(1)}, bf16[14,256,128]{2,1,0:T(8,128)(2,1)}, u32[]{:S(2)}) %copy-start.9) | copy-done | bytes 917528
  48.6 14.0 %shard_map.110 = (f32[1,256]{1,0:T(1,128)S(1)}, bf16[256,2048]{1,0:T(8,128)(2,1)S(1)}, bf16[256,2048]{1,0:T(8,128)(2,1)S(1)}, bf16[256,3328]{1,0:T(8,128)(2,1)S(...) custom-call(s32[26]{0:T(128)S(1)} %copy-done.7, ...), custom_call_target="tpu_custom_call" | custom-call | flops 6979321856 | bytes 13631488 | tf_op jit(solution)/shard_map/pallas_call | solution.py:153
  62.6 0.0 copy-start
  62.7 0.0 copy-start.2
  62.7 0.0 copy-start.6
  62.7 0.6 collective-permute-start.78
  63.3 0.0 collective-permute-done.77.refs_3_
  63.3 0.0 collective-permute-done.76.refs_2_
  63.3 0.0 copy-done.4
  63.3 0.0 copy-done.5
  63.3 7.9 %shard_map.111 = f32[1,256]{1,0:T(1,128)S(1)} custom-call(s32[26]{0:T(128)S(1)} %copy-done.7, bf16[10,256,128]{2,1,0:T(8,128)(2,1)} %get-tuple-element.234.refs_0_, bf16[4,256,128]{2,1,0:T(8,128)(2,1)} %get-tuple-element.235.refs_1_, bf16[10,256,128]{2,1,0:T(8,128)(2,1)S(1)} %collective-permute-done.76.refs_2_, ...), custom_call_target="tpu_custom_call" | custom-call | flops 3489660928 | bytes 13631488 | tf_op jit(solution)/shard_map/pallas_call | solution.py:203
  71.2 0.0 copy-done
  71.2 0.0 copy-done.2
  71.2 11.8 %conditional.5 = (f32[1,256]{1,0:T(1,128)}, f32[1,256]{1,0:T(1,128)}, f32[1,256]{1,0:T(1,128)}) conditional(s32[]{:T(128)} %clamp.2, (f32[1,256]{1,0:T(1,128)S(1)}, f32[1,256]{1,0:T(1,128)S(1)}) %tuple.160, (f32[1,256]{1,0:T(1,128)S(1)}, f32[1,256]{1,0:T(1,128)S(1)}) %tuple.160, (f32[1,256]{1,0:T(1,128)S(1)}, ...), branch_computations={%region_30.0_spmd, %region_31.0_spmd, %region_32.0_spmd, %region_3... | conditional | bytes 12432 | solution.py:307
  71.2 1.5 %collective-permute-start.57 = (f32[1,256]{1,0:T(1,128)S(1)}, f32[1,256]{1,0:T(1,128)}, u32[]{:S(2)}, u32[]{:S(2)}) collective-permute-start(f32[1,256]{1,0:T(1,128)S(1)} %get-tuple-element.140), channel_id=1, source_target_pairs={{0,1},{1,0},{2,3},{3,2},{4,5},{5,4},{6,7},{7,6},{8,9},{9,8},{10,11... | collective-permute-start | bytes 3080 | tf_op jit(solution)/shard_map/cond/branch_9_fun/ppermute | solution.py:288
  72.7 3.8 %collective-permute-start.58 = (f32[1,256]{1,0:T(1,128)S(1)}, f32[1,256]{1,0:T(1,128)}, u32[]{:S(2)}, u32[]{:S(2)}) collective-permute-start(f32[1,256]{1,0:T(1,128)S(1)} %get-tuple-element.141), channel_id=1, source_target_pairs={{0,20},{1,21},{2,22},{3,23},{4,16},{5,17},{6,18},{7,19},{8,28},{9,... | collective-permute-start | bytes 3080 | tf_op jit(solution)/shard_map/cond/branch_9_fun/ppermute | solution.py:298
  76.6 0.0 collective-permute-start.59
  76.6 0.0 collective-permute-done.57
  76.6 1.6 %collective-permute-done.58 = f32[1,256]{1,0:T(1,128)} collective-permute-done((f32[1,256]{1,0:T(1,128)S(1)}, f32[1,256]{1,0:T(1,128)}, u32[]{:S(2)}, u32[]{:S(2)}) %collective-permute-start.58) | collective-permute-done | bytes 1056 | tf_op jit(solution)/shard_map/cond/branch_9_fun/ppermute | solution.py:298
  78.2 4.7 %collective-permute-done.59 = f32[1,256]{1,0:T(1,128)} collective-permute-done((f32[1,256]{1,0:T(1,128)S(1)}, f32[1,256]{1,0:T(1,128)}, u32[]{:S(2)}, u32[]{:S(2)}) %collective-permute-start.59) | collective-permute-done | bytes 1056 | tf_op jit(solution)/shard_map/cond/branch_9_fun/ppermute | solution.py:298
  82.9 0.0 copy-done.6
  82.9 0.0 copy-start.1
  82.9 1.2 %copy-done.1 = bf16[256,2048]{1,0:T(8,128)(2,1)S(1)} copy-done((bf16[256,2048]{1,0:T(8,128)(2,1)S(1)}, bf16[256,2048]{1,0:T(8,128)(2,1)}, u32[]{:S(2)}) %copy-start.1) | copy-done | bytes 1048600
  84.2 0.0 copy-start.3
  84.2 2.5 %shard_map.112 = (bf16[256,2048]{1,0:T(8,128)(2,1)S(1)}, f32[1,2048]{1,0:T(1,128)}, f32[1,2048]{1,0:T(1,128)}, f32[1,1]{1,0:T(1,128)}, f32[1,256]{1,0:T(1,128)S(1)}) custom-call(s32[1,256]{1,0:T(1,128)S(1)} %bitcast.11, f32[1,256]{1,0:T(1,128)S(1)} %get-tuple-element.173.refs_0_, f32[1,256]{1,0:T(1,128)} %get-tuple-element.176.refs_1_, ...), custom_call_target="tpu_custom_call" | custom-call | tf_op jit(solution)/shard_map/pallas_call | solution.py:251
  86.7 7.1 %fusion = bf16[1,3328,2048]{2,1,0:T(8,128)(2,1)} fusion(bf16[256,3328]{1,0:T(8,128)(2,1)S(1)} %get-tuple-element.184, bf16[256,2048]{1,0:T(8,128)(2,1)S(1)} %get-tuple-element.185), kind=kOutput, calls=%fused_computation.1 | convolution fusion | flops 3496476672 | bytes 16384000 | tf_op jit(solution)/shard_map/dot_general | solution.py:343
  93.8 0.0 collective-permute-done.78.refs_1_
  93.8 0.0 copy-done.3
  93.8 2.1 %shard_map.113 = bf16[14,128,256]{2,1,0:T(8,128)(2,1)} custom-call(f32[1,1,256]{2,1,0:T(1,128)S(1)} %bitcast.10, bf16[14,128,256]{2,1,0:T(8,128)(2,1)S(1)} %copy-done.3, bf16[14,128,256]{2,1,0:T(8,128)(2,1)} %collective-permute-done.78.refs_1_), custom_call_target="tpu_custom_call" | custom-call | tf_op jit(solution)/shard_map/pallas_call | solution.py:276
  (1 shorter events, 0.0 us)
Async XLA Ops:
  0.6 45.2 %collective-permute-start.75 = (bf16[14,256,128]{2,1,0:T(8,128)(2,1)}, bf16[14,256,128]{2,1,0:T(8,128)(2,1)S(1)}, u32[]{:S(2)}, u32[]{:S(2)}) collective-permute-start(bf16[14,256,128]{2,1,0:T(8,128)(2,1)} %bitcast.12), channel_id=1, source_target_pairs={{0,1},{1,0},{2,3},{3,2},{4,5},{5,4},{6,7},{7,6},{8,9},{9,8},{10,11... | collective-permute-start | bytes 2752520 | tf_op jit(solution)/shard_map/ppermute | solution.py:288
  2.2 61.1 %copy-start.4 = (bf16[1,2048]{1,0:T(2,128)(2,1)S(1)}, bf16[1,2048]{1,0:T(2,128)(2,1)}, u32[]{:S(2)}) copy-start(bf16[1,2048]{1,0:T(2,128)(2,1)} %refs_5_.1) | copy-start | bytes 12292
  2.2 61.1 %copy-start.5 = (bf16[1,2048]{1,0:T(2,128)(2,1)S(1)}, bf16[1,2048]{1,0:T(2,128)(2,1)}, u32[]{:S(2)}) copy-start(bf16[1,2048]{1,0:T(2,128)(2,1)} %refs_6_.1) | copy-start | bytes 12292
  5.3 28.6 %collective-permute-start.9 = (bf16[10,256,128]{2,1,0:T(8,128)(2,1)S(1)}, bf16[10,256,128]{2,1,0:T(8,128)(2,1)}, u32[]{:S(2)}, u32[]{:S(2)}) collective-permute-start(bf16[10,256,128]{2,1,0:T(8,128)(2,1)S(1)} %param.9), channel_id=1, source_target_pairs={{0,20},{1,21},{2,22},{3,23},{4,16},{5,17},{6,18},{7,19},{8,28},{9,... | collective-permute-start | bytes 1966088 | tf_op jit(solution)/shard_map/cond/branch_9_fun/ppermute | solution.py:298
  33.9 29.4 %collective-permute-start.76 = (bf16[10,256,128]{2,1,0:T(8,128)(2,1)}, bf16[10,256,128]{2,1,0:T(8,128)(2,1)S(1)}, u32[]{:S(2)}, u32[]{:S(2)}) collective-permute-start(bf16[10,256,128]{2,1,0:T(8,128)(2,1)} %get-tuple-element.234.refs_0_), channel_id=1, source_target_pairs={{0,1},{1,0},{2,3},{3,2},{4,5},{5,4},{6,7},{7,6},{8,9},{9,8},{10,11... | collective-permute-start | bytes 1966088 | tf_op jit(solution)/shard_map/ppermute | solution.py:288
  35.4 8.9 %collective-permute-start.24 = (bf16[4,256,128]{2,1,0:T(8,128)(2,1)S(1)}, bf16[4,256,128]{2,1,0:T(8,128)(2,1)}, u32[]{:S(2)}, u32[]{:S(2)}) collective-permute-start(bf16[4,256,128]{2,1,0:T(8,128)(2,1)S(1)} %param.24), channel_id=1, source_target_pairs={{0,20},{1,21},{2,22},{3,23},{4,16},{5,17},{6,18},{7,19},{8,28},{9,... | collective-permute-start | bytes 786440 | tf_op jit(solution)/shard_map/cond/branch_9_fun/ppermute | solution.py:298
  44.3 18.9 %collective-permute-start.77 = (bf16[4,256,128]{2,1,0:T(8,128)(2,1)}, bf16[4,256,128]{2,1,0:T(8,128)(2,1)S(1)}, u32[]{:S(2)}, u32[]{:S(2)}) collective-permute-start(bf16[4,256,128]{2,1,0:T(8,128)(2,1)} %get-tuple-element.235.refs_1_), channel_id=1, source_target_pairs={{0,1},{1,0},{2,3},{3,2},{4,5},{5,4},{6,7},{7,6},{8,9},{9,8},{10,11... | collective-permute-start | bytes 786440 | tf_op jit(solution)/shard_map/ppermute | solution.py:288
  45.8 0.9 copy-start.8
  46.8 0.7 copy-start.7
  47.4 1.2 %copy-start.9 = (bf16[14,256,128]{2,1,0:T(8,128)(2,1)S(1)}, bf16[14,256,128]{2,1,0:T(8,128)(2,1)}, u32[]{:S(2)}) copy-start(bf16[14,256,128]{2,1,0:T(8,128)(2,1)} %copy-done.8) | copy-start | bytes 2752516
  62.6 8.5 %copy-start = (bf16[256,2048]{1,0:T(8,128)(2,1)}, bf16[256,2048]{1,0:T(8,128)(2,1)S(1)}, u32[]{:S(2)}) copy-start(bf16[256,2048]{1,0:T(8,128)(2,1)S(1)} %get-tuple-element.180.refs_5_) | copy-start | bytes 3145732
  62.7 8.5 %copy-start.2 = (bf16[14,128,256]{2,1,0:T(8,128)(2,1)}, bf16[14,128,256]{2,1,0:T(8,128)(2,1)S(1)}, u32[]{:S(2)}) copy-start(bf16[14,128,256]{2,1,0:T(8,128)(2,1)S(1)} %get-tuple-element.182.refs_0_) | copy-start | bytes 2752516
  62.7 20.3 %copy-start.6 = (s32[256]{0:T(256)S(1)}, s32[256]{0:T(256)}, u32[]{:S(2)}) copy-start(s32[256]{0:T(256)} %param.55) | copy-start | bytes 3076
  62.7 31.1 %collective-permute-start.78 = (bf16[14,128,256]{2,1,0:T(8,128)(2,1)}, bf16[14,128,256]{2,1,0:T(8,128)(2,1)}, u32[]{:S(2)}, u32[]{:S(2)}) collective-permute-start(bf16[14,128,256]{2,1,0:T(8,128)(2,1)} %get-tuple-element.183), channel_id=1, source_target_pairs={{0,1},{1,0},{2,3},{3,2},{4,5},{5,4},{6,7},{7,6},{8,9},{9,8},{10,11... | collective-permute-start | bytes 2752520 | tf_op jit(solution)/shard_map/ppermute | solution.py:288
  71.2 5.4 %collective-permute-start.57 = (f32[1,256]{1,0:T(1,128)S(1)}, f32[1,256]{1,0:T(1,128)}, u32[]{:S(2)}, u32[]{:S(2)}) collective-permute-start(f32[1,256]{1,0:T(1,128)S(1)} %get-tuple-element.140), channel_id=1, source_target_pairs={{0,1},{1,0},{2,3},{3,2},{4,5},{5,4},{6,7},{7,6},{8,9},{9,8},{10,11... | collective-permute-start | bytes 3080 | tf_op jit(solution)/shard_map/cond/branch_9_fun/ppermute | solution.py:288
  72.7 5.5 %collective-permute-start.58 = (f32[1,256]{1,0:T(1,128)S(1)}, f32[1,256]{1,0:T(1,128)}, u32[]{:S(2)}, u32[]{:S(2)}) collective-permute-start(f32[1,256]{1,0:T(1,128)S(1)} %get-tuple-element.141), channel_id=1, source_target_pairs={{0,20},{1,21},{2,22},{3,23},{4,16},{5,17},{6,18},{7,19},{8,28},{9,... | collective-permute-start | bytes 3080 | tf_op jit(solution)/shard_map/cond/branch_9_fun/ppermute | solution.py:298
  76.6 6.4 %collective-permute-start.59 = (f32[1,256]{1,0:T(1,128)S(1)}, f32[1,256]{1,0:T(1,128)}, u32[]{:S(2)}, u32[]{:S(2)}) collective-permute-start(f32[1,256]{1,0:T(1,128)S(1)} %get-tuple-element.141), channel_id=1, source_target_pairs={{0,21},{1,20},{2,23},{3,22},{4,17},{5,16},{6,19},{7,18},{8,29},{9,... | collective-permute-start | bytes 3080 | tf_op jit(solution)/shard_map/cond/branch_9_fun/ppermute | solution.py:298
  82.9 1.2 %copy-start.1 = (bf16[256,2048]{1,0:T(8,128)(2,1)S(1)}, bf16[256,2048]{1,0:T(8,128)(2,1)}, u32[]{:S(2)}) copy-start(bf16[256,2048]{1,0:T(8,128)(2,1)} %copy-done) | copy-start | bytes 3145732
  84.2 9.6 %copy-start.3 = (bf16[14,128,256]{2,1,0:T(8,128)(2,1)S(1)}, bf16[14,128,256]{2,1,0:T(8,128)(2,1)}, u32[]{:S(2)}) copy-start(bf16[14,128,256]{2,1,0:T(8,128)(2,1)} %copy-done.2) | copy-start | bytes 2752516
where the time goes:
time: 94.6 us; the launch traced here: 95.9 us
  waiting for transfers between devices  38.1 us (40%)
  Pallas kernels  26.5 us (28%)
  starting transfers between devices  15.3 us (16%)
  local copies, waits for them, and re-layouts  7.38 us (8%)
  matrix products  7.09 us (7%)
  between operations  1.38 us (1%)
    ppermute x4, waiting for transfers between devices, swap(): return lax.ppermute(value, ('copy', 'table'), pairs)  38.1 us
    pallas_call x1, Pallas kernels, student(): pl.pallas_call(functools.partial(student_body, count), in_specs=[SMEM] +...  14 us
    ppermute x4, starting transfers between devices, swap(): return lax.ppermute(value, ('copy', 'table'), pairs)  9.63 us
    pallas_call x1, Pallas kernels, teacher(): pl.pallas_call(functools.partial(teacher_body, pieces), in_specs=[SMEM] +...  7.87 us
    dot_general x1, matrix products, on_device(): lax.dot_general(feats, low, (((0,), (0,)), ((), ())), preferred_element_t...  7.09 us
    ppermute x5, starting transfers between devices, across(): lax.ppermute(value, 'table', [(i, (i + shift) % count) for i in range(cou...  5.7 us
    unnamed x20, local copies, waits for them, and re-layouts  4.01 us
    pallas_call x1, Pallas kernels, row_grads(): pl.pallas_call(functools.partial(rows_body, len(z_parts)), grid=(1,), in_...  2.53 us
  transfers between devices with their start and end apart: 9, of which 4 were waited for; matrix products, arithmetic and copies ran while one was open for 11% of the time, Pallas kernels for 25%

commit v1 on v0

--- a/solution.py
+++ b/solution.py
@@ -7,7 +7,7 @@
 from jax.experimental.pallas import tpu as pltpu
 from jax.sharding import PartitionSpec as P
 
-VMEM_LIMIT = 24 * 1024 * 1024
+VMEM_LIMIT = 10 * 1024 * 1024
 VMEM = pl.BlockSpec(memory_space=pltpu.VMEM)
 SMEM = pl.BlockSpec(memory_space=pltpu.SMEM)
 HBM = pl.BlockSpec(memory_space=pltpu.HBM)
@@ -84,15 +84,18 @@
         total[...] += wide[:, lane : lane + 128]
 
 
-def student_body(count, slot_of, *refs):
-    given, others, refs = refs[:4], refs[4 : 3 + count], refs[3 + count :]
+def student_body(pieces, slot_of, *refs):
+    given, refs = refs[: 3 + len(pieces)], refs[3 + len(pieces) :]
     logit, slope, active, feats, w, *refs = refs
-    grads, (held, total, turned, own, b, h, here, arrived) = refs[:count], refs[count:]
-    slots, emb, _ = grads[0].shape
+    grads = [[refs.pop(0) for _ in sizes] for sizes in pieces]
+    held, total, turned, blocks, b, h, here, arrived = refs
+    emb = grads[0][0].shape[1]
+    slots = blocks.shape[1]
     tile = held.shape[1]
+    wanted = [b, h] + [blocks.at[k] for k in range(len(pieces))]
     small = [
-        pltpu.make_async_copy(source, here_now, here.at[i])
-        for i, (source, here_now) in enumerate(zip(given[1:], (own, b, h)))
+        pltpu.make_async_copy(source, goal, here.at[i])
+        for i, (source, goal) in enumerate(zip(given[1:], wanted))
     ]
     for copy in small:
         copy.start()
@@ -107,7 +110,7 @@
 
     for copy in small:
         copy.wait()
-    copy_features(slot_of, [[own]] + [[other] for other in others], feats)
+    copy_features(slot_of, [[blocks.at[k]] for k in range(len(pieces))], feats)
     total[...] = jnp.zeros_like(total)
 
     def finish(i, pre):
@@ -123,7 +126,7 @@
     forward_tiles(feats, w, b, held, finish, lambda i: fetch(i).wait())
     logit[...] = jnp.sum(total[...].T, axis=0, keepdims=True)
 
-    for grad in grads:
+    for grad in sum(grads, []):
         grad[...] = jnp.zeros_like(grad)
 
     me, tables = lax.axis_index("table"), lax.axis_size("table")
@@ -138,22 +141,30 @@
         for j in range(group):
             slot = slot_of[group * i + j]
             owner = lax.rem(slot // slots + tables - me, tables)
-            for k, grad in enumerate(grads):
-
-                @pl.when(owner == k)
-                def _():
-                    grad[lax.rem(slot, slots)] = value[j * emb : (j + 1) * emb, :]
+            place = lax.rem(slot, slots)
+            for k in range(len(grads)):
+                first = 0
+                for grad in grads[k]:
+                    last = first + grad.shape[0]
+
+                    @pl.when((owner == k) & (place >= first) & (place < last))
+                    def _():
+                        grad[place - first] = value[j * emb : (j + 1) * emb, :]
+
+                    first = last
 
 
 def student(slot_of, blocks, w, b, h):
     slots, rows, emb = blocks[0].shape
     depth, units = w.shape
-    count = len(blocks)
+    halves = [slots // 2] * 2 if slots % 2 == 0 else [slots]
+    pieces = [[slots]] + [halves] * (len(blocks) - 1)
     shape = jax.ShapeDtypeStruct
-    return pl.pallas_call(
-        functools.partial(student_body, count),
-        in_specs=[SMEM] + [HBM] * 4 + [VMEM] * (count - 1),
-        out_specs=[VMEM] * (5 + count),
+    given = [in_hbm(value) for value in (w, b, h, *blocks)]
+    results = pl.pallas_call(
+        functools.partial(student_body, pieces),
+        in_specs=[SMEM] + [HBM] * len(given),
+        out_specs=[VMEM] * (5 + sum(len(sizes) for sizes in pieces)),
         out_shape=[
             shape((1, rows), jnp.float32),
             shape((rows, units), jnp.bfloat16),
@@ -161,15 +172,15 @@
             shape((rows, depth), jnp.bfloat16),
             shape((depth, units), jnp.bfloat16),
         ]
-        + [shape((slots, emb, rows), jnp.bfloat16)] * count,
+        + [shape((size, emb, rows), jnp.bfloat16) for sizes in pieces for size in sizes],
         scratch_shapes=[
             pltpu.VMEM((rows, tiles(units)), jnp.float32),
             pltpu.VMEM((rows, 128), jnp.float32),
             pltpu.VMEM((units, rows), jnp.bfloat16),
-            pltpu.VMEM((slots, rows, emb), jnp.bfloat16),
+            pltpu.VMEM((len(blocks), slots, rows, emb), jnp.bfloat16),
             pltpu.VMEM((1, units), jnp.bfloat16),
             pltpu.VMEM((1, units), jnp.bfloat16),
-            pltpu.SemaphoreType.DMA((3,)),
+            pltpu.SemaphoreType.DMA((2 + len(blocks),)),
             pltpu.SemaphoreType.DMA((units // tiles(units),)),
         ],
         compiler_params=pltpu.CompilerParams(vmem_limit_bytes=VMEM_LIMIT),
@@ -178,7 +189,9 @@
             bytes_accessed=2 * depth * units,
             transcendentals=rows * units,
         ),
-    )(slot_of, *(in_hbm(x) for x in (w, blocks[0], b, h)), *blocks[1:])
+    )(slot_of, *given)
+    grads = list(results[5:])
+    return *results[:5], [[grads.pop(0) for _ in sizes] for sizes in pieces]
 
 
 def teacher_body(pieces, slot_of, *refs):
@@ -264,23 +277,28 @@
     )(labels, *z_parts, *t_parts, slope, active)
 
 
-def scaled_body(count, scale, *refs):
-    total = sum(ref[...].astype(jnp.float32) for ref in refs[:count])
-    refs[count][...] = (total * scale[...]).astype(jnp.bfloat16)
-
-
-def scaled_sum(scale, parts):
-    slots, emb, rows = parts[0].shape
-    group = 7 if slots % 7 == 0 else slots
-    block = pl.BlockSpec((group, emb, rows), lambda i: (i, 0, 0))
+def scaled_body(size, scale, kept, *refs):
+    others, out = refs[:-1], refs[-1]
+    factor = scale[...]
+    for i in range(kept.shape[0] // size):
+        cut = slice(i * size, (i + 1) * size)
+        total = kept[cut].astype(jnp.float32)
+        for pieces in others[i :: kept.shape[0] // size]:
+            total = total + pieces[...].astype(jnp.float32)
+        out[cut] = (total * factor).astype(jnp.bfloat16)
+
+
+def scaled_sum(scale, kept, others):
+    slots, emb, rows = kept.shape
+    size = others[0][0].shape[0]
+    flat = [piece for pieces in others for piece in pieces]
     return pl.pallas_call(
-        functools.partial(scaled_body, len(parts)),
-        grid=(slots // group,),
-        in_specs=[whole((1, 1, rows))] + [block] * len(parts),
-        out_specs=block,
+        functools.partial(scaled_body, size),
+        in_specs=[VMEM] * (2 + len(flat)),
+        out_specs=VMEM,
         out_shape=jax.ShapeDtypeStruct((slots, emb, rows), jnp.bfloat16),
         compiler_params=pltpu.CompilerParams(vmem_limit_bytes=VMEM_LIMIT),
-    )(scale.reshape(1, 1, rows), *parts)
+    )(scale.reshape(1, 1, rows), kept, *flat)
 
 
 def across(value, shift):
@@ -307,10 +325,16 @@
     return lax.switch(distance - 1, branches, *values)
 
 
+def swap_rows(bits, own):
+    cut = (4 * own.shape[0]) // 7
+    first = swap(bits, own[:cut])
+    other = across(own, 1)
+    second = swap(bits, after(own[cut:], first))
+    return other, first, second, across(first, 1)
+
+
 def swap_logits(bits, z_own, t_own):
-    shifts = range(lax.axis_size("table"))
-    t_parts = [swap(bits, t_own, k) for k in shifts]
-    return [z_own] + [across(z_own, k) for k in shifts if k], t_parts
+    return across(z_own, 1), swap(bits, t_own), swap(bits, t_own, 1)
 
 
 def on_device(pooled, slot_of_table, partner, labels, w_first, b_first, w_head):
@@ -320,22 +344,30 @@
     distance = jnp.bitwise_xor(me_copy, partner[me_copy])
 
     own = jnp.transpose(pooled, (1, 0, 2))
-    blocks = [own] + [across(own, k) for k in range(1, tables)]
-    cuts = [0, (5 * slots) // 7, slots] if slots % 7 == 0 else [0, slots]
-    theirs = []
-    for first, last in zip(cuts, cuts[1:]):
-        piece = own[first:last]
-        if theirs:
-            piece = after(piece, theirs[-1])
-        theirs.append(by_distance(swap, distance, piece))
-    their_blocks = [theirs] + [[across(piece, k) for piece in theirs] for k in range(1, tables)]
-
-    z_own, slope, active, feats, w, *parts = student(
+    if tables == 2:
+        other, first, second, first_other = by_distance(swap_rows, distance, own)
+        blocks = [own, other]
+        their_blocks = [[first, second], [first_other, across(second, 1)]]
+    else:
+        theirs = by_distance(swap, distance, own)
+        blocks = [own] + [across(own, k) for k in range(1, tables)]
+        their_blocks = [[theirs]] + [[across(theirs, k)] for k in range(1, tables)]
+
+    z_own, slope, active, feats, w, grads = student(
         slot_of_table, blocks, w_first[0], b_first, w_head
     )
-    parts = parts[:1] + [across(part, k) for k, part in enumerate(parts) if k]
+    early = [across(pieces[0], k) for k, pieces in enumerate(grads) if k]
     t_own = teacher(slot_of_table, their_blocks, w, b_first, w_head)
-    z_parts, t_parts = by_distance(swap_logits, distance, z_own, t_own)
+    if tables == 2:
+        z_other, *t_parts = by_distance(swap_logits, distance, z_own, t_own)
+        z_parts = [z_own, z_other]
+    else:
+        z_own, t_own = lax.psum((z_own, t_own), "table")
+        z_parts, t_parts = [z_own], [by_distance(swap, distance, t_own)]
+    others = [
+        [piece] + [across(after(rest, t_parts[-1]), k) for rest in grads[k][1:]]
+        for k, piece in enumerate(early, 1)
+    ]
 
     low, grad_bias, grad_head, loss, scale = row_grads(
         z_parts, t_parts, labels.reshape(1, rows), slope, active
@@ -343,7 +375,7 @@
     grad_first = lax.dot_general(
         feats, low, (((0,), (0,)), ((), ())), preferred_element_type=jnp.float32
     ).astype(jnp.bfloat16)
-    pooled_grad = scaled_sum(scale, parts)
+    pooled_grad = scaled_sum(scale, grads[0][0], others)
     return (pooled_grad, grad_first[None], grad_bias, grad_head, loss.reshape(1))
 
 

time: 94.6 us -> 94.9 us (level)
  the two profiles are of different devices: /device:TPU:16 before, /device:TPU:12 now
where the time goes in v1:
time: 94.9 us; the launch traced here: 96.7 us
  waiting for transfers between devices  39.7 us (42%)
  Pallas kernels  26.1 us (28%)
  starting transfers between devices  16.6 us (17%)
  matrix products  7.09 us (7%)
  local copies, waits for them, and re-layouts  5.56 us (6%)
  between operations  1.37 us (1%)
    ppermute x4, waiting for transfers between devices, swap(): return lax.ppermute(value, ('copy', 'table'), pairs)  39.7 us
    pallas_call x1, Pallas kernels, student(): pl.pallas_call(functools.partial(student_body, pieces), in_specs=[SMEM] +...  14.4 us
    ppermute x4, starting transfers between devices, swap(): return lax.ppermute(value, ('copy', 'table'), pairs)  10.2 us
    pallas_call x1, Pallas kernels, teacher(): pl.pallas_call(functools.partial(teacher_body, pieces), in_specs=[SMEM] +...  8 us
    dot_general x1, matrix products, on_device(): lax.dot_general(feats, low, (((0,), (0,)), ((), ())), preferred_element_t...  7.09 us
    ppermute x6, starting transfers between devices, across(): lax.ppermute(value, 'table', [(i, (i + shift) % count) for i in range(cou...  6.41 us
    pallas_call x1, Pallas kernels, row_grads(): pl.pallas_call(functools.partial(rows_body, len(z_parts)), grid=(1,), in_...  2.58 us
    unnamed x18, local copies, waits for them, and re-layouts  2.22 us
  transfers between devices with their start and end apart: 10, of which 3 were waited for; matrix products, arithmetic and copies ran while one was open for 8% of the time, Pallas kernels for 26%

profile of v1, /device:TPU:12, one launch (start us, length us, event | category | flops | bytes accessed | tf_op | source)
XLA Modules:
  0.0 96.7 jit_solution(10773628797630433211)
XLA Ops:
  0.6 1.2 %dynamic_slice.3 = s32[1]{0:T(128)} dynamic-slice(s32[16]{0:T(128)} %param.39, s32[]{:T(128)S(6)} %select_n.3), dynamic_slice_sizes={1} | dynamic-slice | bytes 12 | tf_op jit(solution)/shard_map/dynamic_slice | solution.py:344
  2.5 0.0 copy-start.7
  2.5 46.6 %conditional.2 = (bf16[14,256,128]{2,1,0:T(8,128)(2,1)}, bf16[8,256,128]{2,1,0:T(8,128)(2,1)}, bf16[6,256,128]{2,1,0:T(8,128)(2,1)}, bf16[8,256,128]{2,1,0:T(8,128)(2,1)}) conditional(s32[]{:T(128)} %clamp.4, bf16[14,256,128]{2,1,0:T(8,128)(2,1)} %bitcast.12, bf16[14,256,128]{2,1,0:T(8,128)(2,1)} %bitcast.13, ...), branch_computations={%region_0.0_spmd, %region_1.0_spmd, %region_2.0_spmd, %region_3.0_... | conditional | bytes 11272384 | solution.py:325
  2.6 1.1 %slice.80 = bf16[8,256,128]{2,1,0:T(8,128)(2,1)S(1)} slice(bf16[14,256,128]{2,1,0:T(8,128)(2,1)} %param.10), slice={[0:8], [0:256], [0:128]} | slice | bytes 1048576 | tf_op jit(solution)/shard_map/cond/branch_10_fun/slice | solution.py:330
  3.7 2.0 %collective-permute-start.41 = (bf16[8,256,128]{2,1,0:T(8,128)(2,1)S(1)}, bf16[8,256,128]{2,1,0:T(8,128)(2,1)}, u32[]{:S(2)}, u32[]{:S(2)}) collective-permute-start(bf16[8,256,128]{2,1,0:T(8,128)(2,1)S(1)} %slice.80), channel_id=1, source_target_pairs={{0,22},{1,23},{2,20},{3,21},{4,18},{5,19},{6,16},{7,17},{8,30},{9,... | collective-permute-start | bytes 1572872 | tf_op jit(solution)/shard_map/cond/branch_10_fun/ppermute | solution.py:316
  5.7 1.5 %collective-permute-start.40 = (bf16[14,256,128]{2,1,0:T(8,128)(2,1)}, bf16[14,256,128]{2,1,0:T(8,128)(2,1)}, u32[]{:S(2)}, u32[]{:S(2)}) collective-permute-start(bf16[14,256,128]{2,1,0:T(8,128)(2,1)} %param.10), channel_id=1, source_target_pairs={{0,1},{1,0},{2,3},{3,2},{4,5},{5,4},{6,7},{7,6},{8,9},{9,8},{10,11... | collective-permute-start | bytes 2752520 | tf_op jit(solution)/shard_map/cond/branch_10_fun/ppermute | solution.py:306
  7.2 28.9 %collective-permute-done.41 = bf16[8,256,128]{2,1,0:T(8,128)(2,1)} collective-permute-done((bf16[8,256,128]{2,1,0:T(8,128)(2,1)S(1)}, bf16[8,256,128]{2,1,0:T(8,128)(2,1)}, u32[]{:S(2)}, u32[]{:S(2)}) %collective-permute-start.41) | collective-permute-done | bytes 524320 | tf_op jit(solution)/shard_map/cond/branch_10_fun/ppermute | solution.py:316
  36.1 1.5 %collective-permute-start.43 = (bf16[8,256,128]{2,1,0:T(8,128)(2,1)}, bf16[8,256,128]{2,1,0:T(8,128)(2,1)}, u32[]{:S(2)}, u32[]{:S(2)}) collective-permute-start(bf16[8,256,128]{2,1,0:T(8,128)(2,1)} %collective-permute-done.41), channel_id=1, source_target_pairs={{0,1},{1,0},{2,3},{3,2},{4,5},{5,4},{6,7},{7,6},{8,9},{9,8},{10,11... | collective-permute-start | bytes 1572872 | tf_op jit(solution)/shard_map/cond/branch_10_fun/ppermute | solution.py:306
  37.6 1.0 %slice.81 = bf16[6,256,128]{2,1,0:T(8,128)(2,1)S(1)} slice(bf16[14,256,128]{2,1,0:T(8,128)(2,1)} %param.10), slice={[8:14], [0:256], [0:128]} | slice | bytes 786432 | tf_op jit(solution)/shard_map/cond/branch_10_fun/slice | solution.py:332
  38.6 3.6 %collective-permute-start.42 = (bf16[6,256,128]{2,1,0:T(8,128)(2,1)S(1)}, bf16[6,256,128]{2,1,0:T(8,128)(2,1)}, u32[]{:S(2)}, u32[]{:S(2)}) collective-permute-start(bf16[6,256,128]{2,1,0:T(8,128)(2,1)S(1)} %slice.81), channel_id=1, source_target_pairs={{0,22},{1,23},{2,20},{3,21},{4,18},{5,19},{6,16},{7,17},{8,30},{9,... | collective-permute-start | bytes 1179656 | tf_op jit(solution)/shard_map/cond/branch_10_fun/ppermute | solution.py:316
  42.2 6.9 %collective-permute-done.42 = bf16[6,256,128]{2,1,0:T(8,128)(2,1)} collective-permute-done((bf16[6,256,128]{2,1,0:T(8,128)(2,1)S(1)}, bf16[6,256,128]{2,1,0:T(8,128)(2,1)}, u32[]{:S(2)}, u32[]{:S(2)}) %collective-permute-start.42) | collective-permute-done | bytes 393248 | tf_op jit(solution)/shard_map/cond/branch_10_fun/ppermute | solution.py:316
  49.1 0.0 collective-permute-done.40
  49.1 0.0 collective-permute-done.43
  49.2 0.0 copy-start.4
  49.2 0.0 copy-start.5
  49.2 1.6 %collective-permute-start.105 = (bf16[6,256,128]{2,1,0:T(8,128)(2,1)}, bf16[6,256,128]{2,1,0:T(8,128)(2,1)S(1)}, u32[]{:S(2)}, u32[]{:S(2)}) collective-permute-start(bf16[6,256,128]{2,1,0:T(8,128)(2,1)} %get-tuple-element.149.refs_1_), channel_id=1, source_target_pairs={{0,1},{1,0},{2,3},{3,2},{4,5},{5,4},{6,7},{7,6},{8,9},{9,8},{10,11... | collective-permute-start | bytes 1179656 | tf_op jit(solution)/shard_map/ppermute | solution.py:306
  50.8 0.0 copy-done.7
  50.8 14.4 %shard_map.110 = (f32[1,256]{1,0:T(1,128)S(1)}, bf16[256,2048]{1,0:T(8,128)(2,1)S(1)}, bf16[256,2048]{1,0:T(8,128)(2,1)S(1)}, bf16[256,3328]{1,0:T(8,128)(2,1)S(...) custom-call(s32[26]{0:T(128)S(1)} %copy-done.7, ...), custom_call_target="tpu_custom_call" | custom-call | flops 6979321856 | bytes 13631488 | tf_op jit(solution)/shard_map/pallas_call | solution.py:164
  65.1 0.0 copy-start
  65.1 1.0 copy-done
  66.1 0.0 copy-start.2
  66.1 0.0 copy-start.8
  66.1 0.0 copy-start.6
  66.1 0.5 collective-permute-start.106
  66.6 0.0 collective-permute-done.105.refs_3_
  66.6 0.0 copy-done.4
  66.6 0.0 copy-done.5
  66.7 8.0 %shard_map.111 = f32[1,256]{1,0:T(1,128)S(1)} custom-call(s32[26]{0:T(128)S(1)} %copy-done.7, bf16[8,256,128]{2,1,0:T(8,128)(2,1)} %get-tuple-element.148.refs_0_, bf16[6,256,128]{2,1,0:T(8,128)(2,1)} %get-tuple-element.149.refs_1_, bf16[8,256,128]{2,1,0:T(8,128)(2,1)} %get-tuple-element.150.refs_2_, ...), custom_call_target="tpu_custom_call" | custom-call | flops 3489660928 | bytes 13631488 | tf_op jit(solution)/shard_map/pallas_call | solution.py:216
  74.7 0.0 copy-done.2
  74.7 0.0 copy-done.8
  74.7 9.2 %conditional.3 = (f32[1,256]{1,0:T(1,128)}, f32[1,256]{1,0:T(1,128)}, f32[1,256]{1,0:T(1,128)}) conditional(s32[]{:T(128)} %clamp.4, (f32[1,256]{1,0:T(1,128)S(1)}, f32[1,256]{1,0:T(1,128)S(1)}) %tuple.144, (f32[1,256]{1,0:T(1,128)S(1)}, f32[1,256]{1,0:T(1,128)S(1)}) %tuple.144, (f32[1,256]{1,0:T(1,128)S(1)}, ...), branch_computations={%region_15.0_spmd, %region_16.0_spmd, %region_17.0_spmd, %region_1... | conditional | bytes 12432 | solution.py:325
  74.9 3.3 %collective-permute-start.91 = (f32[1,256]{1,0:T(1,128)S(1)}, f32[1,256]{1,0:T(1,128)}, u32[]{:S(2)}, u32[]{:S(2)}) collective-permute-start(f32[1,256]{1,0:T(1,128)S(1)} %get-tuple-element.111), channel_id=1, source_target_pairs={{0,22},{1,23},{2,20},{3,21},{4,18},{5,19},{6,16},{7,17},{8,30},{9,... | collective-permute-start | bytes 3080 | tf_op jit(solution)/shard_map/cond/branch_10_fun/ppermute | solution.py:316
  78.2 1.2 %collective-permute-start.92 = (f32[1,256]{1,0:T(1,128)S(1)}, f32[1,256]{1,0:T(1,128)}, u32[]{:S(2)}, u32[]{:S(2)}) collective-permute-start(f32[1,256]{1,0:T(1,128)S(1)} %get-tuple-element.111), channel_id=1, source_target_pairs={{0,23},{1,22},{2,21},{3,20},{4,19},{5,18},{6,17},{7,16},{8,31},{9,... | collective-permute-start | bytes 3080 | tf_op jit(solution)/shard_map/cond/branch_10_fun/ppermute | solution.py:316
  79.4 0.5 collective-permute-start.90
  80.0 0.0 collective-permute-done.91
  80.0 3.9 %collective-permute-done.92 = f32[1,256]{1,0:T(1,128)} collective-permute-done((f32[1,256]{1,0:T(1,128)S(1)}, f32[1,256]{1,0:T(1,128)}, u32[]{:S(2)}, u32[]{:S(2)}) %collective-permute-start.92) | collective-permute-done | bytes 1056 | tf_op jit(solution)/shard_map/cond/branch_10_fun/ppermute | solution.py:316
  83.8 0.0 collective-permute-done.90
  83.8 0.8 collective-permute-start.107
  84.6 0.0 copy-done.6
  84.6 0.0 copy-start.1
  84.6 1.2 %copy-done.1 = bf16[256,2048]{1,0:T(8,128)(2,1)S(1)} copy-done((bf16[256,2048]{1,0:T(8,128)(2,1)S(1)}, bf16[256,2048]{1,0:T(8,128)(2,1)}, u32[]{:S(2)}) %copy-start.1) | copy-done | bytes 1048600
  85.8 0.0 copy-start.3
  85.8 2.6 %shard_map.112 = (bf16[256,2048]{1,0:T(8,128)(2,1)S(1)}, f32[1,2048]{1,0:T(1,128)}, f32[1,2048]{1,0:T(1,128)}, f32[1,1]{1,0:T(1,128)}, f32[1,256]{1,0:T(1,128)S(1)}) custom-call(s32[1,256]{1,0:T(1,128)S(1)} %bitcast.11, f32[1,256]{1,0:T(1,128)S(1)} %get-tuple-element.147.refs_0_, f32[1,256]{1,0:T(1,128)} %get-tuple-element.152.refs_1_, ...), custom_call_target="tpu_custom_call" | custom-call | tf_op jit(solution)/shard_map/pallas_call | solution.py:264
  88.4 7.1 %fusion = bf16[1,3328,2048]{2,1,0:T(8,128)(2,1)} fusion(bf16[256,3328]{1,0:T(8,128)(2,1)S(1)} %get-tuple-element.162, bf16[256,2048]{1,0:T(8,128)(2,1)S(1)} %get-tuple-element.163), kind=kOutput, calls=%fused_computation.1 | convolution fusion | flops 3496476672 | bytes 16384000 | tf_op jit(solution)/shard_map/dot_general | solution.py:375
  95.5 0.0 collective-permute-done.106.refs_0_
  95.5 0.0 collective-permute-done.107.refs_1_
  95.5 0.0 copy-done.3
  95.5 1.2 %shard_map.113 = bf16[14,128,256]{2,1,0:T(8,128)(2,1)} custom-call(f32[1,1,256]{2,1,0:T(1,128)S(1)} %bitcast.10, bf16[14,128,256]{2,1,0:T(8,128)(2,1)S(1)} %copy-done.3, bf16[7,128,256]{2,1,0:T(8,128)(2,1)S(1)} %collective-permute-done.106.refs_0_, bf16[7,128,256]{2,1,0:T(8,128)(2,1)S(1)} %collective-permute-done.107.refs_1_), custom_call_target="tpu_custom_call" | custom-call | tf_op jit(solution)/shard_map/pallas_call | solution.py:295
Async XLA Ops:
  2.5 48.2 %copy-start.7 = (s32[26]{0:T(128)S(1)}, s32[26]{0:T(128)}, u32[]{:S(2)}) copy-start(s32[26]{0:T(128)} %slot_of.3) | copy-start | bytes 316
  3.7 32.4 %collective-permute-start.41 = (bf16[8,256,128]{2,1,0:T(8,128)(2,1)S(1)}, bf16[8,256,128]{2,1,0:T(8,128)(2,1)}, u32[]{:S(2)}, u32[]{:S(2)}) collective-permute-start(bf16[8,256,128]{2,1,0:T(8,128)(2,1)S(1)} %slice.80), channel_id=1, source_target_pairs={{0,22},{1,23},{2,20},{3,21},{4,18},{5,19},{6,16},{7,17},{8,30},{9,... | collective-permute-start | bytes 1572872 | tf_op jit(solution)/shard_map/cond/branch_10_fun/ppermute | solution.py:316
  5.7 43.4 %collective-permute-start.40 = (bf16[14,256,128]{2,1,0:T(8,128)(2,1)}, bf16[14,256,128]{2,1,0:T(8,128)(2,1)}, u32[]{:S(2)}, u32[]{:S(2)}) collective-permute-start(bf16[14,256,128]{2,1,0:T(8,128)(2,1)} %param.10), channel_id=1, source_target_pairs={{0,1},{1,0},{2,3},{3,2},{4,5},{5,4},{6,7},{7,6},{8,9},{9,8},{10,11... | collective-permute-start | bytes 2752520 | tf_op jit(solution)/shard_map/cond/branch_10_fun/ppermute | solution.py:306
  36.1 13.0 %collective-permute-start.43 = (bf16[8,256,128]{2,1,0:T(8,128)(2,1)}, bf16[8,256,128]{2,1,0:T(8,128)(2,1)}, u32[]{:S(2)}, u32[]{:S(2)}) collective-permute-start(bf16[8,256,128]{2,1,0:T(8,128)(2,1)} %collective-permute-done.41), channel_id=1, source_target_pairs={{0,1},{1,0},{2,3},{3,2},{4,5},{5,4},{6,7},{7,6},{8,9},{9,8},{10,11... | collective-permute-start | bytes 1572872 | tf_op jit(solution)/shard_map/cond/branch_10_fun/ppermute | solution.py:306
  38.6 10.5 %collective-permute-start.42 = (bf16[6,256,128]{2,1,0:T(8,128)(2,1)S(1)}, bf16[6,256,128]{2,1,0:T(8,128)(2,1)}, u32[]{:S(2)}, u32[]{:S(2)}) collective-permute-start(bf16[6,256,128]{2,1,0:T(8,128)(2,1)S(1)} %slice.81), channel_id=1, source_target_pairs={{0,22},{1,23},{2,20},{3,21},{4,18},{5,19},{6,16},{7,17},{8,30},{9,... | collective-permute-start | bytes 1179656 | tf_op jit(solution)/shard_map/cond/branch_10_fun/ppermute | solution.py:316
  49.2 17.5 %copy-start.4 = (bf16[1,2048]{1,0:T(2,128)(2,1)S(1)}, bf16[1,2048]{1,0:T(2,128)(2,1)}, u32[]{:S(2)}) copy-start(bf16[1,2048]{1,0:T(2,128)(2,1)} %refs_5_.1) | copy-start | bytes 12292
  49.2 17.5 %copy-start.5 = (bf16[1,2048]{1,0:T(2,128)(2,1)S(1)}, bf16[1,2048]{1,0:T(2,128)(2,1)}, u32[]{:S(2)}) copy-start(bf16[1,2048]{1,0:T(2,128)(2,1)} %refs_6_.1) | copy-start | bytes 12292
  49.2 17.5 %collective-permute-start.105 = (bf16[6,256,128]{2,1,0:T(8,128)(2,1)}, bf16[6,256,128]{2,1,0:T(8,128)(2,1)S(1)}, u32[]{:S(2)}, u32[]{:S(2)}) collective-permute-start(bf16[6,256,128]{2,1,0:T(8,128)(2,1)} %get-tuple-element.149.refs_1_), channel_id=1, source_target_pairs={{0,1},{1,0},{2,3},{3,2},{4,5},{5,4},{6,7},{7,6},{8,9},{9,8},{10,11... | collective-permute-start | bytes 1179656 | tf_op jit(solution)/shard_map/ppermute | solution.py:306
  65.1 1.0 %copy-start = (bf16[256,2048]{1,0:T(8,128)(2,1)}, bf16[256,2048]{1,0:T(8,128)(2,1)S(1)}, u32[]{:S(2)}) copy-start(bf16[256,2048]{1,0:T(8,128)(2,1)S(1)} %get-tuple-element.156.refs_5_) | copy-start | bytes 3145732
  66.1 8.6 %copy-start.2 = (bf16[14,128,256]{2,1,0:T(8,128)(2,1)}, bf16[14,128,256]{2,1,0:T(8,128)(2,1)S(1)}, u32[]{:S(2)}) copy-start(bf16[14,128,256]{2,1,0:T(8,128)(2,1)S(1)} %get-tuple-element.158.kept) | copy-start | bytes 2752516
  66.1 8.6 %copy-start.8 = (bf16[7,128,256]{2,1,0:T(8,128)(2,1)}, bf16[7,128,256]{2,1,0:T(8,128)(2,1)S(1)}, u32[]{:S(2)}) copy-start(bf16[7,128,256]{2,1,0:T(8,128)(2,1)S(1)} %get-tuple-element.161) | copy-start | bytes 1376260
  66.1 18.5 %copy-start.6 = (s32[256]{0:T(256)S(1)}, s32[256]{0:T(256)}, u32[]{:S(2)}) copy-start(s32[256]{0:T(256)} %param.40) | copy-start | bytes 3076
  66.1 29.4 %collective-permute-start.106 = (bf16[7,128,256]{2,1,0:T(8,128)(2,1)}, bf16[7,128,256]{2,1,0:T(8,128)(2,1)S(1)}, u32[]{:S(2)}, u32[]{:S(2)}) collective-permute-start(bf16[7,128,256]{2,1,0:T(8,128)(2,1)} %get-tuple-element.159), channel_id=1, source_target_pairs={{0,1},{1,0},{2,3},{3,2},{4,5},{5,4},{6,7},{7,6},{8,9},{9,8},{10,11... | collective-permute-start | bytes 1376264 | tf_op jit(solution)/shard_map/ppermute | solution.py:306
  74.9 5.1 %collective-permute-start.91 = (f32[1,256]{1,0:T(1,128)S(1)}, f32[1,256]{1,0:T(1,128)}, u32[]{:S(2)}, u32[]{:S(2)}) collective-permute-start(f32[1,256]{1,0:T(1,128)S(1)} %get-tuple-element.111), channel_id=1, source_target_pairs={{0,22},{1,23},{2,20},{3,21},{4,18},{5,19},{6,16},{7,17},{8,30},{9,... | collective-permute-start | bytes 3080 | tf_op jit(solution)/shard_map/cond/branch_10_fun/ppermute | solution.py:316
  78.2 5.6 %collective-permute-start.92 = (f32[1,256]{1,0:T(1,128)S(1)}, f32[1,256]{1,0:T(1,128)}, u32[]{:S(2)}, u32[]{:S(2)}) collective-permute-start(f32[1,256]{1,0:T(1,128)S(1)} %get-tuple-element.111), channel_id=1, source_target_pairs={{0,23},{1,22},{2,21},{3,20},{4,19},{5,18},{6,17},{7,16},{8,31},{9,... | collective-permute-start | bytes 3080 | tf_op jit(solution)/shard_map/cond/branch_10_fun/ppermute | solution.py:316
  79.4 4.4 %collective-permute-start.90 = (f32[1,256]{1,0:T(1,128)S(1)}, f32[1,256]{1,0:T(1,128)}, u32[]{:S(2)}, u32[]{:S(2)}) collective-permute-start(f32[1,256]{1,0:T(1,128)S(1)} %get-tuple-element.110), channel_id=1, source_target_pairs={{0,1},{1,0},{2,3},{3,2},{4,5},{5,4},{6,7},{7,6},{8,9},{9,8},{10,11... | collective-permute-start | bytes 3080 | tf_op jit(solution)/shard_map/cond/branch_10_fun/ppermute | solution.py:306
  83.8 11.7 %collective-permute-start.107 = (bf16[7,128,256]{2,1,0:T(8,128)(2,1)}, bf16[7,128,256]{2,1,0:T(8,128)(2,1)S(1)}, u32[]{:S(2)}, u32[]{:S(2)}) collective-permute-start(bf16[7,128,256]{2,1,0:T(8,128)(2,1)} %copy-done.8), channel_id=1, source_target_pairs={{0,1},{1,0},{2,3},{3,2},{4,5},{5,4},{6,7},{7,6},{8,9},{9,8},{10,11... | collective-permute-start | bytes 1376264 | tf_op jit(solution)/shard_map/ppermute | solution.py:306
  84.6 1.2 %copy-start.1 = (bf16[256,2048]{1,0:T(8,128)(2,1)S(1)}, bf16[256,2048]{1,0:T(8,128)(2,1)}, u32[]{:S(2)}) copy-start(bf16[256,2048]{1,0:T(8,128)(2,1)} %copy-done) | copy-start | bytes 3145732
  85.8 9.7 %copy-start.3 = (bf16[14,128,256]{2,1,0:T(8,128)(2,1)S(1)}, bf16[14,128,256]{2,1,0:T(8,128)(2,1)}, u32[]{:S(2)}) copy-start(bf16[14,128,256]{2,1,0:T(8,128)(2,1)} %copy-done.2) | copy-start | bytes 2752516
